TPU v7x, 32 devices: a whole 2x2x4 slice. The times are simulated.
32 devices in a mesh: row: 4 (over x, core), col: 8 (over z, y).
Axes of the slice: x: 2, y: 2, z: 4, core: 2. Of those that a mesh axis runs over, the one named last changes fastest.
Arguments:
- activations: bfloat16 [256, 5120], P('col', 'row'), may hold values from -1.5 to 1.5
- grad_output: bfloat16 [256, 5120], P('col', 'row'), may hold values from -1.5 to 1.5
- gate_pre: bfloat16 [256, 25600], P('row', 'col'), may hold values from -6 to 6
- up_pre: bfloat16 [256, 25600], P('row', 'col'), may hold values from -6 to 6
- gate_weight: bfloat16 [5120, 25600], P('row', 'col'), may hold values from -0.078125 to 0.078125
- up_weight: bfloat16 [5120, 25600], P('row', 'col'), may hold values from -0.078125 to 0.078125
- down_weight: bfloat16 [25600, 5120], P('col', 'row'), may hold values from -0.0390625 to 0.0390625
Outputs:
- grad_input: float32 [256, 5120], P('col', 'row')
- grad_gate_weight: float32 [5120, 25600], P('row', 'col')
- grad_up_weight: float32 [5120, 25600], P('row', 'col')
- grad_down_weight: float32 [25600, 5120], P('col', 'row')
All inputs are finite; a program needn't handle non-finite values.
Results may differ from a plain program's by a relative error of at most 0.0029.
Values may be sent and summed in bfloat16 or wider, within the bound.
A program may use at most 128 MiB of HBM per device.

v0:
```python
import jax
import jax.numpy as jnp
from jax import lax
from jax.sharding import PartitionSpec as P


def swiglu_back(gate_vals, up_vals, grad_hidden):
    gate_wide = gate_vals.astype(jnp.float32)
    up_wide = up_vals.astype(jnp.float32)
    logistic = jax.nn.sigmoid(gate_wide)
    silu_val = gate_wide * logistic
    hidden = (silu_val * up_wide).astype(jnp.bfloat16)
    grad_gate = (grad_hidden * up_wide * logistic * (1.0 + gate_wide * (1.0 - logistic))).astype(
        jnp.bfloat16
    )
    grad_up = (grad_hidden * silu_val).astype(jnp.bfloat16)
    return (hidden, grad_gate, grad_up)


def right_trans(left, right):
    return lax.dot_general(
        left, right, (((1,), (1,)), ((), ())), preferred_element_type=jnp.float32
    )


def left_trans(left, right):
    return lax.dot_general(
        left, right, (((0,), (0,)), ((), ())), preferred_element_type=jnp.float32
    )


def shards(activations, grad_output, gate_pre, up_pre, gate_weight, up_weight, down_weight):
    grad_rows = lax.all_gather(grad_output, "col", axis=0, tiled=True)
    segment = grad_rows
    own_hidden = lax.psum_scatter(
        right_trans(segment, down_weight), "row", scatter_dimension=0, tiled=True
    )
    local_h, local_gate, local_up = swiglu_back(gate_pre, up_pre, own_hidden)
    hidden, grad_gate, grad_up = (
        lax.all_gather(local_h, "row", axis=0, tiled=True),
        lax.all_gather(local_gate, "row", axis=0, tiled=True),
        lax.all_gather(local_up, "row", axis=0, tiled=True),
    )
    grad_down_weight = left_trans(hidden, grad_rows)
    segment = lax.all_gather(activations, "col", axis=0, tiled=True)
    gate_slice = grad_gate
    up_slice = grad_up
    grad_gate_weight = left_trans(segment, gate_slice)
    grad_up_weight = left_trans(segment, up_slice)
    gate_slice = grad_gate
    up_slice = grad_up
    grad_input = lax.psum_scatter(
        right_trans(gate_slice, gate_weight) + right_trans(up_slice, up_weight),
        "col",
        scatter_dimension=0,
        tiled=True,
    )
    return (grad_input, grad_gate_weight, grad_up_weight, grad_down_weight)


def solution(mesh):
    placed = (
        P("col", "row"),
        P("col", "row"),
        P("row", "col"),
        P("row", "col"),
        P("row", "col"),
        P("row", "col"),
        P("col", "row"),
    )
    return jax.shard_map(
        shards,
        mesh=mesh,
        in_specs=placed,
        out_specs=(P("col", "row"), P("row", "col"), P("row", "col"), P("col", "row")),
        check_vma=False,
    )
```

profile of v0, /device:TPU:0, one launch (start us, length us, event | category | flops | bytes accessed | tf_op | source)
XLA Modules:
  0.0 242.2 jit_solution(8822980137809711645)
XLA Ops:
  7.2 0.0 reduce-scatter.3.cloned.1.call-start
  7.2 33.6 %all_gather.15 = bf16[256,1280]{1,0:T(8,128)(2,1)S(1)} all-gather(bf16[32,1280]{1,0:T(8,128)(2,1)} %param.8), channel_id=1, replica_groups=mesh['row'=4,'col'=8] {'col'}, dimensions={0}, use_global_device_ids=true | all-gather | bytes 737280 | tf_op jit(solution)/shard_map/all_gather | solution.py:33
  40.8 7.4 %fusion.8 = f32[256,3200]{1,0:T(8,128)} fusion(bf16[256,1280]{1,0:T(8,128)(2,1)S(1)} %all_gather.15, bf16[3200,1280]{1,0:T(8,128)(2,1)} %param.13), kind=kOutput, calls=%fused_computation.17 | convolution fusion | flops 2097152000 | bytes 12124160 | tf_op jit(solution)/shard_map/dot_general | solution.py:21
  48.2 0.0 copy-start.2
  48.2 0.0 copy-start.3
  48.2 0.0 reduce-scatter.3.cloned.1.call-update
  48.3 0.0 all-gather.4.cloned.1.call-start
  48.3 39.9 %reduce-scatter.3.cloned.1.call-done = f32[64,3200]{1,0:T(8,128)} async-done(((f32[256,3200]{1,0:T(8,128)}), f32[64,3200]{1,0:T(8,128)}) %reduce-scatter.3.cloned.1.call-update) | async-done | bytes 819216 | tf_op jit(solution)/shard_map/reduce_scatter | solution.py:35
  88.2 0.0 copy-done.2
  88.2 0.0 copy-done.3
  88.2 2.6 %multiply_convert_fusion = (bf16[64,3200]{1,0:T(8,128)(2,1)}, bf16[64,3200]{1,0:T(8,128)(2,1)}, bf16[64,3200]{1,0:T(8,128)(2,1)}) fusion(f32[64,3200]{1,0:T(8,128)} %reduce-scatter.3.cloned.1.call-done, bf16[64,3200]{1,0:T(8,128)(2,1)S(1)} %copy-done.2, bf16[64,3200]{1,0:T(8,128)(2,1)S(1)} %copy-done.3), kind=kLoop, calls=%fused_computation.16 | loop fusion | flops 3481600 | bytes 2867200 | tf_op jit(solution)/shard_map/convert_element_type | solution.py:16
  90.8 0.0 all-gather.4.cloned.1.call-update
  90.8 0.0 all-gather.6.cloned.1.call-start
  90.9 0.7 all-gather.6.cloned.1.call-update
  91.6 0.0 all-gather.8.cloned.1.call-start
  91.6 0.5 all-gather.8.cloned.1.call-update
  92.2 0.0 reduce-scatter.5.cloned.1.call-start
  92.2 18.8 %all-gather.4.cloned.1.call-done = bf16[256,3200]{1,0:T(8,128)(2,1)} async-done(((bf16[64,3200]{1,0:T(8,128)(2,1)}), bf16[256,3200]{1,0:T(8,128)(2,1)}) %all-gather.4.cloned.1.call-update) | async-done | bytes 1638416 | tf_op jit(solution)/shard_map/all_gather | solution.py:41
  111.0 6.2 %fusion.9 = f32[256,1280]{1,0:T(8,128)S(1)} fusion(bf16[256,3200]{1,0:T(8,128)(2,1)} %all-gather.4.cloned.1.call-done, bf16[1280,3200]{1,0:T(8,128)(2,1)} %param.11), kind=kOutput, calls=%fused_computation.18 | convolution fusion | flops 2097152000 | bytes 11141120 | tf_op jit(solution)/shard_map/dot_general | solution.py:21
  117.2 0.0 copy-start.4
  117.3 16.0 %all-gather.6.cloned.1.call-done = bf16[256,3200]{1,0:T(8,128)(2,1)} async-done(((bf16[64,3200]{1,0:T(8,128)(2,1)}), bf16[256,3200]{1,0:T(8,128)(2,1)}) %all-gather.6.cloned.1.call-update) | async-done | bytes 1638416 | tf_op jit(solution)/shard_map/all_gather | solution.py:42
  133.3 7.3 %convolution_add_fusion = f32[256,1280]{1,0:T(8,128)} fusion(f32[256,1280]{1,0:T(8,128)S(1)} %fusion.9, bf16[256,3200]{1,0:T(8,128)(2,1)} %all-gather.6.cloned.1.call-done, bf16[1280,3200]{1,0:T(8,128)(2,1)} %param.12), kind=kOutput, calls=%fused_computation.2 | convolution fusion | flops 2097479680 | bytes 12451840 | tf_op jit(solution)/shard_map/dot_general | solution.py:21
  140.6 0.0 reduce-scatter.5.cloned.1.call-update
  140.6 0.0 copy-done.4
  140.6 32.4 %all_gather.18 = bf16[256,1280]{1,0:T(8,128)(2,1)S(1)} all-gather(bf16[32,1280]{1,0:T(8,128)(2,1)S(1)} %copy-done.4), channel_id=1, replica_groups=mesh['row'=4,'col'=8] {'col'}, dimensions={0}, use_global_device_ids=true | all-gather | bytes 737280 | tf_op jit(solution)/shard_map/all_gather | solution.py:45
  173.1 0.0 copy-done
  173.1 8.4 %convolution_bitcast_fusion.1 = f32[1280,3200]{0,1:T(8,128)} fusion(bf16[256,3200]{1,0:T(8,128)(2,1)S(1)} %copy-done, bf16[256,1280]{1,0:T(8,128)(2,1)S(1)} %all_gather.18), kind=kOutput, calls=%fused_computation.1 | convolution fusion | flops 2097152000 | bytes 18677760 | tf_op jit(solution)/shard_map/dot_general | solution.py:27
  181.4 18.1 %copy.11 = f32[1280,3200]{1,0:T(8,128)} copy(f32[1280,3200]{0,1:T(8,128)} %convolution_bitcast_fusion.1) | data formatting | bytes 32768000
  199.6 0.0 copy-done.1
  199.6 8.4 %convolution_bitcast_fusion = f32[1280,3200]{0,1:T(8,128)} fusion(bf16[256,3200]{1,0:T(8,128)(2,1)S(1)} %copy-done.1, bf16[256,1280]{1,0:T(8,128)(2,1)S(1)} %all_gather.18), kind=kOutput, calls=%fused_computation | convolution fusion | flops 2097152000 | bytes 18677760 | tf_op jit(solution)/shard_map/dot_general | solution.py:27
  207.9 18.0 %copy.12 = f32[1280,3200]{1,0:T(8,128)} copy(f32[1280,3200]{0,1:T(8,128)} %convolution_bitcast_fusion) | data formatting | bytes 32768000
  225.9 9.8 %fusion.10 = f32[3200,1280]{1,0:T(8,128)} fusion(bf16[256,3200]{1,0:T(8,128)(2,1)} %all-gather.8.cloned.1.call-done, bf16[256,1280]{1,0:T(8,128)(2,1)S(1)} %all_gather.15), kind=kOutput, calls=%fused_computation.19 | convolution fusion | flops 2097152000 | bytes 18677760 | tf_op jit(solution)/shard_map/dot_general | solution.py:27
  (4 shorter events, 0.0 us)
Async XLA Ops:
  7.2 81.1 %reduce-scatter.3.cloned.1.call-start = ((), (), s32[]{:S(2)}) async-start(), calls=%async_computation.2 | async-start | bytes 4096000 | tf_op jit(solution)/shard_map/reduce_scatter | solution.py:35
  48.2 40.0 %copy-start.2 = (bf16[64,3200]{1,0:T(8,128)(2,1)S(1)}, bf16[64,3200]{1,0:T(8,128)(2,1)}, u32[]{:S(2)}) copy-start(bf16[64,3200]{1,0:T(8,128)(2,1)} %param.9) | copy-start | bytes 1228804
  48.2 40.0 %copy-start.3 = (bf16[64,3200]{1,0:T(8,128)(2,1)S(1)}, bf16[64,3200]{1,0:T(8,128)(2,1)}, u32[]{:S(2)}) copy-start(bf16[64,3200]{1,0:T(8,128)(2,1)} %param.10) | copy-start | bytes 1228804
  48.3 62.7 %all-gather.4.cloned.1.call-start = ((), (), s32[]{:S(2)}) async-start(), calls=%async_computation.3 | async-start | bytes 2048000 | tf_op jit(solution)/shard_map/all_gather | solution.py:41
  90.8 42.5 %all-gather.6.cloned.1.call-start = ((), (), s32[]{:S(2)}) async-start(), calls=%async_computation.4 | async-start | bytes 2048000 | tf_op jit(solution)/shard_map/all_gather | solution.py:42
  91.6 134.3 %all-gather.8.cloned.1.call-start = ((), (), s32[]{:S(2)}) async-start(), calls=%async_computation.6 | async-start | bytes 2048000 | tf_op jit(solution)/shard_map/all_gather | solution.py:40
  92.2 143.6 %reduce-scatter.5.cloned.1.call-start = ((), (), s32[]{:S(2)}) async-start(), calls=%async_computation.5 | async-start | bytes 1474560 | tf_op jit(solution)/shard_map/reduce_scatter | solution.py:52
  117.2 23.4 %copy-start.4 = (bf16[32,1280]{1,0:T(8,128)(2,1)S(1)}, bf16[32,1280]{1,0:T(8,128)(2,1)}, u32[]{:S(2)}) copy-start(bf16[32,1280]{1,0:T(8,128)(2,1)} %param.7) | copy-start | bytes 245764
  140.6 32.5 %copy-start = (bf16[256,3200]{1,0:T(8,128)(2,1)S(1)}, bf16[256,3200]{1,0:T(8,128)(2,1)}, u32[]{:S(2)}) copy-start(bf16[256,3200]{1,0:T(8,128)(2,1)} %all-gather.4.cloned.1.call-done) | copy-start | bytes 4915204
  181.4 18.1 %copy-start.1 = (bf16[256,3200]{1,0:T(8,128)(2,1)S(1)}, bf16[256,3200]{1,0:T(8,128)(2,1)}, u32[]{:S(2)}) copy-start(bf16[256,3200]{1,0:T(8,128)(2,1)} %all-gather.6.cloned.1.call-done) | copy-start | bytes 4915204
Sparse Core Ops, SparseCore 0:
  48.4 39.7 reduce-scatter.2
  91.0 20.0 all-gather.3
  113.2 20.0 all-gather.5
  134.8 20.0 all-gather.7
  159.0 64.4 reduce-scatter.4
where the time goes:
time: 243 us; the launch traced here: 242 us
  waiting for transfers between devices  76 us (31%)
  blocking collectives  66 us (27%)
  matrix products  47.6 us (20%)
  local copies, waits for them, and re-layouts  36.1 us (15%)
  between operations  13.8 us (6%)
  other arithmetic  2.57 us (1%)
    reduce_scatter x1, waiting for transfers between devices, shards(): lax.psum_scatter(right_trans(segment, down_weight), 'row', scatter_dimens...  39.9 us
    unnamed x12, local copies, waits for them, and re-layouts  36.1 us
    all_gather x1, blocking collectives, shards(): grad_rows = lax.all_gather(grad_output, 'col', axis=0, tiled=True)  33.6 us
    all_gather x1, blocking collectives, shards(): segment = lax.all_gather(activations, 'col', axis=0, tiled=True)  32.4 us
    dot_general x3, matrix products, left_trans(): lax.dot_general(left, right, (((0,), (0,)), ((), ())), preferred_element_...  26.6 us
    dot_general x3, matrix products, right_trans(): lax.dot_general(left, right, (((1,), (1,)), ((), ())), preferred_element_...  21 us
    all_gather x1, waiting for transfers between devices, shards(): lax.all_gather(local_gate, 'row', axis=0, tiled=True)  18.8 us
    all_gather x1, waiting for transfers between devices, shards(): lax.all_gather(local_up, 'row', axis=0, tiled=True)  16 us
  transfers between devices with their start and end apart: 5, of which 3 were waited for; matrix products, arithmetic and copies ran while one was open for 31% of the time, Pallas kernels for 0%

commit v1 on v0

v1 whole, which is shorter than its diff:
```python
import functools

import jax
import jax.numpy as jnp
from jax import lax
from jax.experimental import pallas as pl
from jax.experimental.pallas import tpu as pltpu
from jax.sharding import PartitionSpec as P

MESH = pl.DeviceIdType.MESH
VMEM = pl.BlockSpec(memory_space=pltpu.VMEM)


def right_trans(left, right):
    return lax.dot_general(
        left, right, (((1,), (1,)), ((), ())), preferred_element_type=jnp.float32
    )


class Gather:
    def __init__(self, buf, axis, size, block, send_sem, recv_sem, base):
        self.buf, self.axis, self.half, self.block = buf, axis, size // 2, block
        self.send_sem, self.recv_sem, self.base = send_sem, recv_sem, base
        self.me = lax.axis_index(axis)
        self.major, self.minor = self.me // 2, self.me % 2
        self.slots = size - 1

    def view(self, index, cols):
        start = pl.multiple_of(index * self.block, self.block)
        return self.buf.at[pl.ds(start, self.block), cols]

    def copy(self, index, target, slot, cols, at):
        sem = self.base + at * self.slots + slot
        return pltpu.make_async_remote_copy(
            src_ref=self.view(index, cols),
            dst_ref=self.view(index, cols),
            send_sem=self.send_sem.at[sem],
            recv_sem=self.recv_sem.at[sem],
            device_id={self.axis: target},
            device_id_type=MESH,
        )

    def pair(self):
        return self.major * 2 + 1 - self.minor

    def to_pair(self, cols, at):
        return self.copy(self.me, self.pair(), 0, cols, at)

    def to_peer(self, k, cols, at):
        target = lax.rem(self.major + k, self.half) * 2 + self.minor
        return self.copy(self.me, target, k, cols, at)

    def onward(self, k, cols, at):
        source = lax.rem(self.major - k + self.half, self.half) * 2 + self.minor
        return self.copy(source, self.pair(), self.half - 1 + k, cols, at)

    def start(self, cols=slice(None), at=0):
        for k in range(1, self.half):
            self.to_peer(k, cols, at).start()
        self.to_pair(cols, at).start()

    def forward(self, cols=slice(None), at=0):
        for k in range(1, self.half):
            self.to_peer(k, cols, at).wait_recv()
            self.onward(k, cols, at).start()

    def arrive(self, cols=slice(None), at=0):
        self.to_pair(cols, at).wait_recv()
        for k in range(1, self.half):
            self.onward(k, cols, at).wait_recv()

    def drain(self, cols=slice(None), at=0):
        self.to_pair(cols, at).wait_send()
        for k in range(1, self.half):
            self.to_peer(k, cols, at).wait_send()
            self.onward(k, cols, at).wait_send()


def middle_kernel(
    rows_n, cols_n, chunks,
    go_ref, act_ref, gate_ref, up_ref, down_hbm,
    go_all, act_all, hid_all, gg_all, gu_all,
    down, partial, sib, xsend, xrecv, own, send_sem, recv_sem, local_sem,
):
    half = rows_n // 2
    width_tokens = go_ref.shape[0]
    hidden_tokens, units = gate_ref.shape
    wide = units // chunks
    row = lax.axis_index("row")
    major, minor = row // 2, row % 2
    pair = major * 2 + 1 - minor

    load = pltpu.make_async_copy(down_hbm, down, local_sem)
    load.start()

    def cols(j):
        if chunks == 1:
            return slice(None)
        return pl.ds(pl.multiple_of(j * wide, wide), wide)

    base = 0
    go = Gather(go_all, "col", cols_n, width_tokens, send_sem, recv_sem, base)
    base += cols_n - 1
    act = Gather(act_all, "col", cols_n, width_tokens, send_sem, recv_sem, base)
    base += cols_n - 1
    hid = Gather(hid_all, "row", rows_n, hidden_tokens, send_sem, recv_sem, base)
    base += rows_n - 1
    gg = Gather(gg_all, "row", rows_n, hidden_tokens, send_sem, recv_sem, base)
    base += chunks * (rows_n - 1)
    gu = Gather(gu_all, "row", rows_n, hidden_tokens, send_sem, recv_sem, base)
    base += chunks * (rows_n - 1)
    sib_base = base
    base += chunks
    x_base = base

    barrier = pltpu.get_barrier_semaphore()
    for plan in (go, hid):
        pl.semaphore_signal(
            barrier, inc=1, device_id={plan.axis: plan.pair()}, device_id_type=MESH
        )
        for k in range(1, plan.half):
            target = lax.rem(plan.major + k, plan.half) * 2 + plan.minor
            pl.semaphore_signal(
                barrier, inc=1, device_id={plan.axis: target}, device_id_type=MESH
            )
    pl.semaphore_wait(barrier, cols_n // 2 + half)

    go_at = pl.ds(pl.multiple_of(go.me * width_tokens, width_tokens), width_tokens)
    go_all[go_at, :] = go_ref[...]
    go.start()

    row_at = pl.ds(pl.multiple_of(row * hidden_tokens, hidden_tokens), hidden_tokens)

    def hidden_step(j, carry):
        gate = gate_ref[:, cols(j)].astype(jnp.float32)
        up = up_ref[:, cols(j)].astype(jnp.float32)
        silu = gate * jax.nn.sigmoid(gate)
        hid_all[row_at, cols(j)] = (silu * up).astype(jnp.bfloat16)
        return carry

    lax.fori_loop(0, chunks, hidden_step, 0)
    hid.start()

    go.forward()
    act_all[go_at, :] = act_ref[...]
    act.start()
    load.wait()
    go.arrive()

    def sib_copy(j):
        return pltpu.make_async_remote_copy(
            src_ref=partial.at[:, 1 - minor, :, cols(j)],
            dst_ref=sib.at[:, :, cols(j)],
            send_sem=send_sem.at[sib_base + j],
            recv_sem=recv_sem.at[sib_base + j],
            device_id={"row": pair},
            device_id_type=MESH,
        )

    def x_copy(k, j):
        target = lax.rem(major + k, half) * 2 + minor
        sem = x_base + j * (half - 1) + k - 1
        return pltpu.make_async_remote_copy(
            src_ref=xsend.at[k - 1, :, cols(j)],
            dst_ref=xrecv.at[k - 1, :, cols(j)],
            send_sem=send_sem.at[sem],
            recv_sem=recv_sem.at[sem],
            device_id={"row": target},
            device_id_type=MESH,
        )

    def product_step(j, carry):
        if chunks == 1:
            weight = down[...]
        else:
            weight = down[pl.ds(pl.multiple_of(j * wide, wide), wide), :]
        total = right_trans(go_all[...], weight)
        partial[:, :, :, cols(j)] = total.reshape(half, 2, hidden_tokens, wide)
        sib_copy(j).start()
        return carry

    lax.fori_loop(0, chunks, product_step, 0)

    def pair_step(j, carry):
        sib_copy(j).wait_recv()
        for k in range(1, half):
            block = lax.rem(major + k, half)
            total = partial[block, minor, :, cols(j)] + sib[block, :, cols(j)]
            xsend[k - 1, :, cols(j)] = total.astype(jnp.bfloat16)
            x_copy(k, j).start()
        own[:, cols(j)] = partial[major, minor, :, cols(j)] + sib[major, :, cols(j)]
        return carry

    lax.fori_loop(0, chunks, pair_step, 0)

    hid.forward()
    act.forward()

    def grad_step(j, carry):
        grad = own[:, cols(j)]
        for k in range(1, half):
            x_copy(k, j).wait_recv()
            grad = grad + xrecv[k - 1, :, cols(j)].astype(jnp.float32)
        gate = gate_ref[:, cols(j)].astype(jnp.float32)
        up = up_ref[:, cols(j)].astype(jnp.float32)
        logistic = jax.nn.sigmoid(gate)
        gg_all[row_at, cols(j)] = (
            grad * up * logistic * (1.0 + gate * (1.0 - logistic))
        ).astype(jnp.bfloat16)
        gg.start(cols(j), j)
        gu_all[row_at, cols(j)] = (grad * (gate * logistic)).astype(jnp.bfloat16)
        gu.start(cols(j), j)
        return carry

    lax.fori_loop(0, chunks, grad_step, 0)

    def pass_step(j, carry):
        gg.forward(cols(j), j)
        gu.forward(cols(j), j)
        return carry

    lax.fori_loop(0, chunks, pass_step, 0)

    act.arrive()
    hid.arrive()
    go.drain()
    act.drain()
    hid.drain()

    def end_step(j, carry):
        for plan in (gg, gu):
            plan.arrive(cols(j), j)
            plan.drain(cols(j), j)
        sib_copy(j).wait_send()
        for k in range(1, half):
            x_copy(k, j).wait_send()
        return carry

    lax.fori_loop(0, chunks, end_step, 0)


def middle(rows_n, cols_n, grad_output, activations, gate_pre, up_pre, down_weight):
    width_tokens, features = grad_output.shape
    hidden_tokens, units = gate_pre.shape
    tokens = width_tokens * cols_n
    chunks = 5 if units % 640 == 0 else 1
    half = rows_n // 2
    sems = 2 * (cols_n - 1) + (1 + 2 * chunks) * (rows_n - 1) + chunks * half
    narrow = jax.ShapeDtypeStruct((tokens, features), jnp.bfloat16)
    broad = jax.ShapeDtypeStruct((tokens, units), jnp.bfloat16)
    peers = max(half - 1, 1)
    return pl.pallas_call(
        functools.partial(middle_kernel, rows_n, cols_n, chunks),
        out_shape=(narrow, narrow, broad, broad, broad),
        in_specs=[VMEM] * 4 + [pl.BlockSpec(memory_space=pl.ANY)],
        out_specs=(VMEM,) * 5,
        scratch_shapes=[
            pltpu.VMEM((units, features), jnp.bfloat16),
            pltpu.VMEM((half, 2, hidden_tokens, units), jnp.float32),
            pltpu.VMEM((half, hidden_tokens, units), jnp.float32),
            pltpu.VMEM((peers, hidden_tokens, units), jnp.bfloat16),
            pltpu.VMEM((peers, hidden_tokens, units), jnp.bfloat16),
            pltpu.VMEM((hidden_tokens, units), jnp.float32),
            pltpu.SemaphoreType.DMA((sems,)),
            pltpu.SemaphoreType.DMA((sems,)),
            pltpu.SemaphoreType.DMA,
        ],
        compiler_params=pltpu.CompilerParams(
            collective_id=0, has_side_effects=True, vmem_limit_bytes=48 * 1024 * 1024
        ),
        cost_estimate=pl.CostEstimate(
            flops=2 * tokens * features * units,
            bytes_accessed=2 * units * features,
            transcendentals=0,
        ),
    )(grad_output, activations, gate_pre, up_pre, down_weight)


def outer_kernel(left_ref, right_ref, out_ref):
    out_ref[...] = lax.dot_general(
        left_ref[...],
        right_ref[...],
        (((0,), (0,)), ((), ())),
        preferred_element_type=jnp.float32,
    )


def left_trans(left, right):
    tokens, height = left.shape
    width = right.shape[1]
    tile = height
    for steps in (10, 5, 4, 2):
        if height % (128 * steps) == 0 and (height // steps) * width >= 2**19:
            tile = height // steps
            break
    return pl.pallas_call(
        outer_kernel,
        grid=(height // tile,),
        out_shape=jax.ShapeDtypeStruct((height, width), jnp.float32),
        in_specs=[
            pl.BlockSpec((tokens, tile), lambda i: (0, i)),
            pl.BlockSpec((tokens, width), lambda i: (0, 0)),
        ],
        out_specs=pl.BlockSpec((tile, width), lambda i: (i, 0)),
        compiler_params=pltpu.CompilerParams(vmem_limit_bytes=40 * 1024 * 1024),
        cost_estimate=pl.CostEstimate(
            flops=2 * tokens * height * width,
            bytes_accessed=4 * height * width + 2 * tokens * (height + width),
            transcendentals=0,
        ),
    )(left, right)


def shards(
    rows_n, cols_n,
    activations, grad_output, gate_pre, up_pre, gate_weight, up_weight, down_weight,
):
    grad_rows, act_rows, hidden, grad_gate, grad_up = middle(
        rows_n, cols_n, grad_output, activations, gate_pre, up_pre, down_weight
    )
    share = right_trans(grad_gate, gate_weight) + right_trans(grad_up, up_weight)
    share, grad_rows, act_rows, hidden, grad_gate, grad_up = lax.optimization_barrier(
        (share, grad_rows, act_rows, hidden, grad_gate, grad_up)
    )
    grad_input = lax.psum_scatter(share, "col", scatter_dimension=0, tiled=True)
    grad_gate_weight = left_trans(act_rows, grad_gate)
    grad_up_weight = left_trans(act_rows, grad_up)
    grad_down_weight = left_trans(hidden, grad_rows)
    return (grad_input, grad_gate_weight, grad_up_weight, grad_down_weight)


def solution(mesh):
    placed = (
        P("col", "row"),
        P("col", "row"),
        P("row", "col"),
        P("row", "col"),
        P("row", "col"),
        P("row", "col"),
        P("col", "row"),
    )
    return jax.shard_map(
        functools.partial(shards, mesh.shape["row"], mesh.shape["col"]),
        mesh=mesh,
        in_specs=placed,
        out_specs=(P("col", "row"), P("row", "col"), P("row", "col"), P("col", "row")),
        check_vma=False,
    )
```

time: 243 us -> 141 us (0.58)
  Pallas kernels: 0 us -> 73.2 us
  blocking collectives: 66 us -> 0 us
  matrix products: 47.6 us -> 5.85 us
  waiting for transfers between devices: 76 us -> 40.1 us
  local copies, waits for them, and re-layouts: 36.1 us -> 7.18 us
  other arithmetic: 2.57 us -> 0 us
    pallas_call x0 -> x4, Pallas kernels: none -> 73.2 us  [the longest x1 51.8 us: middle(): pl.pallas_call(functools.partial(middle_kernel, rows_n, cols_n, chunks),...]
    all_gather x2 -> x0, blocking collectives: 66 us -> none  [the longest x1 33.6 us: shards(): grad_rows = lax.all_gather(grad_output, 'col', axis=0, tiled=True)]
    all_gather x3 -> x0, waiting for transfers between devices: 34.8 us -> none  [the longest x1 18.8 us: shards(): lax.all_gather(local_gate, 'row', axis=0, tiled=True)]
    unnamed x12 -> x20, local copies, waits for them, and re-layouts: 36.1 us -> 7.18 us
    dot_general x3 -> x0, matrix products: 26.6 us -> none  [left_trans(): lax.dot_general(left, right, (((0,), (0,)), ((), ())), preferred_element_...]
    dot_general x3 -> x2, matrix products: 21 us -> 5.85 us  [right_trans(): lax.dot_general(left, right, (((1,), (1,)), ((), ())), preferred_element_...]
    convert_element_type x1 -> x0, other arithmetic: 2.57 us -> none  [swiglu_back(): grad_up = (grad_hidden * silu_val).astype(jnp.bfloat16)]
    reduce_scatter x2 -> x1, waiting for transfers between devices: 39.9 us -> 40.1 us  [shards(): grad_input = lax.psum_scatter(share, 'col', scatter_dimension=0, tiled=True)]
  transfers between devices with their start and end apart: 5 -> 1, of which waited for: 3 -> 1; matrix products, arithmetic and copies ran while one was open for 31% -> 0% of each run, Pallas kernels for 0% -> 15%
where the time goes in v1:
time: 141 us; the launch traced here: 140 us
  Pallas kernels  73.2 us (52%)
  waiting for transfers between devices  40.1 us (28%)
  between operations  14.1 us (10%)
  local copies, waits for them, and re-layouts  7.18 us (5%)
  matrix products  5.85 us (4%)
    pallas_call x1, Pallas kernels, middle(): pl.pallas_call(functools.partial(middle_kernel, rows_n, cols_n, chunks),...  51.8 us
    reduce_scatter x1, waiting for transfers between devices, shards(): grad_input = lax.psum_scatter(share, 'col', scatter_dimension=0, tiled=True)  40.1 us
    pallas_call x3, Pallas kernels, left_trans(): pl.pallas_call(outer_kernel, grid=(height // tile,), out_shape=jax.ShapeD...  21.4 us
    unnamed x20, local copies, waits for them, and re-layouts  7.18 us
    dot_general x2, matrix products, right_trans(): lax.dot_general(left, right, (((1,), (1,)), ((), ())), preferred_element_...  5.85 us
  transfers between devices with their start and end apart: 1, of which 1 were waited for; matrix products, arithmetic and copies ran while one was open for 0% of the time, Pallas kernels for 15%

profile of v1, /device:TPU:0, one launch (start us, length us, event | category | flops | bytes accessed | tf_op | source)
XLA Modules:
  0.0 140.5 jit_solution(11027842220656174672)
XLA Ops:
  7.2 0.0 reduce-scatter.2.cloned.1.call-start
  7.2 0.0 copy-start.4
  7.2 1.0 copy-done.4
  8.2 0.0 copy-start.5
  8.2 1.0 copy-done.5
  9.2 0.0 copy-start.6
  9.2 0.9 copy-done.6
  10.1 0.0 copy-start.7
  10.1 0.9 copy-done.7
  11.0 0.0 copy-start.8
  11.0 51.8 %shard_map.102 = (bf16[256,1280]{1,0:T(8,128)(2,1)S(1)}, bf16[256,1280]{1,0:T(8,128)(2,1)S(1)}, bf16[256,3200]{1,0:T(8,128)(2,1)S(1)}, bf16[256,3200]{1,0:T(8,128)(2,1)S(1)}, bf16[256,3200]{1,0:T(8,128)(2,1)}) custom-call(bf16[32,1280]{1,0:T(8,128)(2,1)S(1)} %copy-done.6, bf16[32,1280]{1,0:T(8,128)(2,1)S(1)} %copy-done.7, bf16[64,3200]{1,0:T(8,128)(2,1)S(1)} %copy-done.4, ...), custom_call_target="tpu_custom_call" | custom-call | flops 2097152000 | bytes 8192000 | tf_op jit(solution)/shard_map/pallas_call | solution.py:252
  62.8 0.0 copy-start.2
  62.8 0.0 copy-done.8
  62.9 0.0 copy-start
  62.9 0.0 copy-start.9
  62.9 2.4 %fusion = f32[256,1280]{1,0:T(8,128)S(1)} fusion(bf16[256,3200]{1,0:T(8,128)(2,1)S(1)} %get-tuple-element.22.right_ref, bf16[1280,3200]{1,0:T(8,128)(2,1)S(1)} %copy-done.8), kind=kOutput, calls=%fused_computation.1 | convolution fusion | flops 2097152000 | bytes 11141120 | tf_op jit(solution)/shard_map/dot_general | solution.py:15
  65.3 0.0 copy-done.2
  65.3 0.0 copy-done
  65.3 2.0 %copy-done.9 = bf16[1280,3200]{1,0:T(8,128)(2,1)S(1)} copy-done((bf16[1280,3200]{1,0:T(8,128)(2,1)S(1)}, bf16[1280,3200]{1,0:T(8,128)(2,1)}, u32[]{:S(2)}) %copy-start.9) | copy-done | bytes 8192024
  67.3 3.5 %convolution_add_fusion = f32[256,1280]{1,0:T(8,128)} fusion(f32[256,1280]{1,0:T(8,128)S(1)} %fusion, bf16[256,3200]{1,0:T(8,128)(2,1)S(1)} %copy-done, bf16[1280,3200]{1,0:T(8,128)(2,1)S(1)} %copy-done.9), kind=kOutput, calls=%fused_computation | convolution fusion | flops 2097479680 | bytes 12451840 | tf_op jit(solution)/shard_map/dot_general | solution.py:15
  70.7 0.0 reduce-scatter.2.cloned.1.call-update
  70.8 0.0 copy-start.3
  70.8 1.4 %copy-done.3 = bf16[256,3200]{1,0:T(8,128)(2,1)S(1)} copy-done((bf16[256,3200]{1,0:T(8,128)(2,1)S(1)}, bf16[256,3200]{1,0:T(8,128)(2,1)}, u32[]{:S(2)}) %copy-start.3) | copy-done | bytes 1638424
  72.2 0.0 copy-start.1
  72.2 7.1 %shard_map.103 = f32[1280,3200]{1,0:T(8,128)} custom-call(bf16[256,1280]{1,0:T(8,128)(2,1)S(1)} %get-tuple-element.21.left_ref, bf16[256,3200]{1,0:T(8,128)(2,1)S(1)} %copy-done.3), custom_call_target="tpu_custom_call" | custom-call | flops 2097152000 | bytes 18677760 | tf_op jit(solution)/shard_map/pallas_call | solution.py:296
  79.3 0.0 copy-done.1
  79.3 7.1 %shard_map.104 = f32[1280,3200]{1,0:T(8,128)} custom-call(bf16[256,1280]{1,0:T(8,128)(2,1)S(1)} %get-tuple-element.21.left_ref, bf16[256,3200]{1,0:T(8,128)(2,1)S(1)} %copy-done.1), custom_call_target="tpu_custom_call" | custom-call | flops 2097152000 | bytes 18677760 | tf_op jit(solution)/shard_map/pallas_call | solution.py:296
  86.4 7.2 %shard_map.105 = f32[3200,1280]{1,0:T(8,128)} custom-call(bf16[256,3200]{1,0:T(8,128)(2,1)S(1)} %get-tuple-element.24.left_ref, bf16[256,1280]{1,0:T(8,128)(2,1)S(1)} %get-tuple-element.25.right_ref), custom_call_target="tpu_custom_call" | custom-call | flops 2097152000 | bytes 18677760 | tf_op jit(solution)/shard_map/pallas_call | solution.py:296
  93.5 40.1 %reduce-scatter.2.cloned.1.call-done = f32[32,1280]{1,0:T(8,128)} async-done(((f32[256,1280]{1,0:T(8,128)}), f32[32,1280]{1,0:T(8,128)}) %reduce-scatter.2.cloned.1.call-update) | async-done | bytes 163856 | tf_op jit(solution)/shard_map/reduce_scatter | solution.py:325
Async XLA Ops:
  7.2 126.5 %reduce-scatter.2.cloned.1.call-start = ((), (), s32[]{:S(2)}) async-start(), calls=%async_computation.1 | async-start | bytes 1474560 | tf_op jit(solution)/shard_map/reduce_scatter | solution.py:325
  7.2 1.0 copy-start.4
  8.2 1.0 copy-start.5
  9.2 0.9 copy-start.6
  10.1 0.9 copy-start.7
  11.0 51.9 %copy-start.8 = (bf16[1280,3200]{1,0:T(8,128)(2,1)S(1)}, bf16[1280,3200]{1,0:T(8,128)(2,1)}, u32[]{:S(2)}) copy-start(bf16[1280,3200]{1,0:T(8,128)(2,1)} %param.11) | copy-start | bytes 24576004
  62.8 2.4 %copy-start.2 = (bf16[256,3200]{1,0:T(8,128)(2,1)}, bf16[256,3200]{1,0:T(8,128)(2,1)S(1)}, u32[]{:S(2)}) copy-start(bf16[256,3200]{1,0:T(8,128)(2,1)S(1)} %get-tuple-element.22.right_ref) | copy-start | bytes 4915204
  62.9 2.4 %copy-start = (bf16[256,3200]{1,0:T(8,128)(2,1)S(1)}, bf16[256,3200]{1,0:T(8,128)(2,1)}, u32[]{:S(2)}) copy-start(bf16[256,3200]{1,0:T(8,128)(2,1)} %get-tuple-element.23.right_ref) | copy-start | bytes 4915204
  62.9 4.4 %copy-start.9 = (bf16[1280,3200]{1,0:T(8,128)(2,1)S(1)}, bf16[1280,3200]{1,0:T(8,128)(2,1)}, u32[]{:S(2)}) copy-start(bf16[1280,3200]{1,0:T(8,128)(2,1)} %param.12) | copy-start | bytes 24576004
  70.8 1.4 %copy-start.3 = (bf16[256,3200]{1,0:T(8,128)(2,1)S(1)}, bf16[256,3200]{1,0:T(8,128)(2,1)}, u32[]{:S(2)}) copy-start(bf16[256,3200]{1,0:T(8,128)(2,1)} %copy-done.2) | copy-start | bytes 4915204
  72.2 7.1 %copy-start.1 = (bf16[256,3200]{1,0:T(8,128)(2,1)S(1)}, bf16[256,3200]{1,0:T(8,128)(2,1)}, u32[]{:S(2)}) copy-start(bf16[256,3200]{1,0:T(8,128)(2,1)} %get-tuple-element.23.right_ref) | copy-start | bytes 4915204
Sparse Core Ops, SparseCore 0:
  70.9 62.7 reduce-scatter.1
